TPU v7x, 32 devices: a whole 2x2x4 slice. The times are simulated.
32 devices in a mesh: dp: 4 (over y, x), expert: 8 (over z, core).
Axes of the slice: x: 2, y: 2, z: 4, core: 2. Of those that a mesh axis runs over, the one named last changes fastest.
Arguments:
- tokens: bfloat16 [8, 1024, 1024], P('expert', 'dp'), may hold values from -6 to 6
- cotangent: bfloat16 [8, 1024, 1024], P('expert', 'dp'), may hold values from -6 to 6
- lengths: int32 [8], P('expert'), may hold values from 128 to 1024, as said below
- picks: int32 [8, 1024, 8, 2], P('expert', 'dp'), may hold values from 0 to 4, all different within a row
- routes: int32 [8, 1024, 16], P('expert', 'dp'), may hold values from 0 to 95, all different within a row; in each aligned block of 256 rows (0 to 255, 256 to 511, ..., all dimensions but the last counted through in order) at most 77 rows name the same one
- qk_weight: float32 [1024, 1024], P(('dp', 'expert')), may hold values from -0.25 to 0.25
- qk_first: float32 [1024, 1024], P(('dp', 'expert')), may hold values from -192 to 192
- qk_second: float32 [1024, 1024], P(('dp', 'expert')), may hold values from 1884.16 to 31129.6
- value_weight: float32 [1024, 2560], P(('dp', 'expert')), may hold values from -0.1875 to 0.1875
- value_first: float32 [1024, 2560], P(('dp', 'expert')), may hold values from -64 to 64
- value_second: float32 [1024, 2560], P(('dp', 'expert')), may hold values from 212.992 to 3440.64
- output_weight: float32 [1024, 2560], P(('dp', 'expert')), may hold values from -10 to 10
- output_first: float32 [1024, 2560], P(('dp', 'expert')), may hold values from -0.75 to 0.75
- output_second: float32 [1024, 2560], P(('dp', 'expert')), may hold values from 0.0303104 to 0.49152
- select_weight: float32 [1024, 40], P(('dp', 'expert')), may hold values from -0.1875 to 0.1875
- select_first: float32 [1024, 40], P(('dp', 'expert')), may hold values from -320 to 320
- select_second: float32 [1024, 40], P(('dp', 'expert')), may hold values from 5324.8 to 86016
- router_weight: float32 [1024, 96], P(('dp', 'expert')), may hold values from -0.09375 to 0.09375
- router_first: float32 [1024, 96], P(('dp', 'expert')), may hold values from -64 to 64
- router_second: float32 [1024, 96], P(('dp', 'expert')), may hold values from 313.95 to 5187
- gain_weight: float32 [1024], P(('dp', 'expert')), may hold values from 0.4 to 1.6
- gain_first: float32 [1024], P(('dp', 'expert')), may hold values from -768 to 768
- gain_second: float32 [1024], P(('dp', 'expert')), may hold values from 15099.494 to 964689.92
- expert_weight: float32 [96, 1024, 256], P('expert', 'dp'), may hold values from -0.3125 to 0.3125
- expert_first: float32 [96, 1024, 256], P('expert', 'dp'), may hold values from -12 to 12
- expert_second: float32 [96, 1024, 256], P('expert', 'dp'), may hold values from 8.8725 to 143.325
Outputs:
- layer_out: bfloat16 [8, 1024, 1024], P('expert', 'dp')
- input_grad: float32 [8, 1024, 1024], P('expert', 'dp')
- qk_new: float32 [1024, 1024], P(('dp', 'expert'))
- qk_first_new: float32 [1024, 1024], P(('dp', 'expert'))
- qk_second_new: float32 [1024, 1024], P(('dp', 'expert'))
- value_new: float32 [1024, 2560], P(('dp', 'expert'))
- value_first_new: float32 [1024, 2560], P(('dp', 'expert'))
- value_second_new: float32 [1024, 2560], P(('dp', 'expert'))
- output_new: float32 [1024, 2560], P(('dp', 'expert'))
- output_first_new: float32 [1024, 2560], P(('dp', 'expert'))
- output_second_new: float32 [1024, 2560], P(('dp', 'expert'))
- select_new: float32 [1024, 40], P(('dp', 'expert'))
- select_first_new: float32 [1024, 40], P(('dp', 'expert'))
- select_second_new: float32 [1024, 40], P(('dp', 'expert'))
- router_new: float32 [1024, 96], P(('dp', 'expert'))
- router_first_new: float32 [1024, 96], P(('dp', 'expert'))
- router_second_new: float32 [1024, 96], P(('dp', 'expert'))
- gain_new: float32 [1024], P(('dp', 'expert'))
- gain_first_new: float32 [1024], P(('dp', 'expert'))
- gain_second_new: float32 [1024], P(('dp', 'expert'))
- expert_new: float32 [96, 1024, 256], P('expert', 'dp')
- expert_first_new: float32 [96, 1024, 256], P('expert', 'dp')
- expert_second_new: float32 [96, 1024, 256], P('expert', 'dp')
- expert_counts: int32 [96], replicated
Inputs may be any that keep to these rules, and one draw needn't show every extreme that they name: `lengths`: A sequence has 128 to 1024 valid positions at its start; some sequence has all 1024. `picks`: two different experts for each head's value projection and for its output projection. `routes`: each token names 16 different experts; the 256 rows of one device name no expert more than 77 times, a bound that some block reaches.
All inputs are finite; a program needn't handle non-finite values.
Results may differ from a plain program's by a relative error of at most 0.02.
The roundings to bfloat16 on the way count: a program that leaves them out, or rounds other values in their place, can miss the bound.
Values may be sent and summed in bfloat16 or wider, within the bound.
No kernel may reach another device: no remote copies, remote signals or barrier semaphores. Data moves between devices by JAX's collectives and lax.ppermute only.
A program may use at most 320 MiB of HBM per device.

v0:
```python
import jax
import jax.numpy as jnp
from jax import lax
from jax.sharding import PartitionSpec as P

HEADS = 4
HEAD_DIM = 128
ATT_EXPERTS = 5
EXPERT_H = 128
TOPK = 16
STEP = 10


norm_eps = 1e-05
beta_first = 0.9
beta_second = 0.95
adam_eps = 1e-08
weight_decay = 0.1
masked_score = -1e30
rope_base = 10000.0
rate_query_key = 0.04
rate_value = 0.03
rate_output = 2.0
rate_select = 0.03
rate_router = 0.015
rate_gain = 1.2
rate_expert = 0.05


def product(former, latter):
    return jnp.dot(former, latter, preferred_element_type=jnp.float32)


def product_rows(former, latter):
    return lax.dot_general(
        former, latter, (((0,), (0,)), ((), ())), preferred_element_type=jnp.float32
    )


def product_last(former, latter):
    return lax.dot_general(
        former, latter, (((1,), (1,)), ((), ())), preferred_element_type=jnp.float32
    )


def layer_norm(values, gain_row):
    center = values - jnp.mean(values, axis=-1, keepdims=True)
    spread = jnp.mean(center * center, axis=-1, keepdims=True)
    return center * lax.rsqrt(spread + norm_eps) * gain_row


def norm_backward(values, gain_row, upstream):
    center = values - jnp.mean(values, axis=-1, keepdims=True)
    inverse = lax.rsqrt(jnp.mean(center * center, axis=-1, keepdims=True) + norm_eps)
    scaled = center * inverse
    gain_grad = jnp.sum(upstream * scaled, axis=0)
    through = upstream * gain_row
    input_grad = inverse * (
        through
        - jnp.mean(through, axis=-1, keepdims=True)
        - scaled * jnp.mean(through * scaled, axis=-1, keepdims=True)
    )
    return (input_grad, gain_grad)


def rope_tables(positions, head_size):
    half_size = head_size // 2
    frequency = jnp.exp(-jnp.log(rope_base) * jnp.arange(half_size).astype(jnp.float32) / half_size)
    angles = positions[:, None] * frequency[None, :]
    return (jnp.cos(angles)[:, None, :], jnp.sin(angles)[:, None, :])


def rotate(head_rows, cosine, sine_table, direction):
    half_size = head_rows.shape[-1] // 2
    leading = head_rows[..., :half_size]
    trailing = head_rows[..., half_size:]
    return jnp.concatenate(
        [
            leading * cosine - direction * trailing * sine_table,
            direction * leading * sine_table + trailing * cosine,
        ],
        axis=-1,
    )


def silu_slope(inner):
    sigma = jax.nn.sigmoid(inner)
    return sigma * (1.0 + inner * (1.0 - sigma))


def adamw_update(weight, first_moment, second_moment, gradient, rate):
    first_new = beta_first * first_moment + (1.0 - beta_first) * gradient
    second_new = beta_second * second_moment + (1.0 - beta_second) * gradient * gradient
    first_hat = first_new / (1.0 - beta_first**STEP)
    second_hat = second_new / (1.0 - beta_second**STEP)
    weight_new = weight - rate * (
        first_hat / (jnp.sqrt(second_hat) + adam_eps) + weight_decay * weight
    )
    return (weight_new, first_new, second_new)


def local(
    tokens,
    cotangent,
    lengths,
    picks,
    routes,
    qk_weight,
    qk_first,
    qk_second,
    value_weight,
    value_first,
    value_second,
    output_weight,
    output_first,
    output_second,
    select_weight,
    select_first,
    select_second,
    router_weight,
    router_first,
    router_second,
    gain_weight,
    gain_first,
    gain_second,
    expert_weight,
    expert_first,
    expert_second,
):
    row_count = tokens.shape[1]
    model_width = tokens.shape[2]
    group_count = lax.axis_size("dp")
    owner_count = lax.axis_size("expert")
    local_count = expert_weight.shape[0]
    expert_total = local_count * owner_count
    capacity = (9 * row_count * TOPK + 5 * expert_total - 1) // (5 * expert_total)
    bucket_rows = row_count * group_count
    score_scale = HEAD_DIM ** (-0.5)
    head_width = HEADS * HEAD_DIM
    mixed_width = HEADS * ATT_EXPERTS * HEAD_DIM
    gathered = (
        lax.all_gather(qk_weight.astype(jnp.bfloat16), ("dp", "expert"), axis=0, tiled=True),
        lax.all_gather(value_weight.astype(jnp.bfloat16), ("dp", "expert"), axis=0, tiled=True),
        lax.all_gather(output_weight.astype(jnp.bfloat16), ("dp", "expert"), axis=0, tiled=True),
        lax.all_gather(select_weight.astype(jnp.bfloat16), ("dp", "expert"), axis=0, tiled=True),
        lax.all_gather(router_weight.astype(jnp.bfloat16), ("dp", "expert"), axis=0, tiled=True),
        lax.all_gather(gain_weight.astype(jnp.bfloat16), ("dp", "expert"), axis=0, tiled=True),
    )
    qk_full, value_full, output_full, select_full, router_full, gain_full = gathered
    sequence = tokens[0]
    route_rows = routes[0]
    share = local_count // group_count
    owner_of = route_rows // local_count
    within = route_rows % local_count
    place_ids = (within // share * owner_count + owner_of) * share + within % share
    expert_local = lax.all_to_all(
        expert_weight.astype(jnp.bfloat16), "dp", split_axis=0, concat_axis=1, tiled=True
    )
    expert_in = expert_local[:, :, :EXPERT_H]
    expert_out = expert_local[:, :, EXPERT_H:]
    gain_one = gain_full.astype(jnp.float32)
    inputs_f = sequence.astype(jnp.float32)
    pick_rows = picks[0]
    seq_len = lengths[0]
    offset = lax.axis_index("dp") * row_count
    query_place = offset + jnp.arange(row_count, dtype=jnp.int32)
    valid = query_place < seq_len
    cosine, sine_table = rope_tables(query_place.astype(jnp.float32), HEAD_DIM)
    normed_low = layer_norm(inputs_f, gain_one).astype(jnp.bfloat16)
    query_key = product(normed_low, qk_full).reshape(row_count, 2, HEADS, HEAD_DIM)
    queries = rotate(query_key[:, 0], cosine, sine_table, 1.0).astype(jnp.bfloat16)
    key_rows = rotate(query_key[:, 1], cosine, sine_table, 1.0).astype(jnp.bfloat16)
    chosen = jnp.sum(
        (pick_rows[..., None] == jnp.arange(ATT_EXPERTS, dtype=jnp.int32)).astype(jnp.float32),
        axis=-2,
    )
    chosen = chosen.reshape(row_count, 2, HEADS, ATT_EXPERTS)
    selection = product(normed_low, select_full).reshape(row_count, 2, HEADS, ATT_EXPERTS)
    sigma_sel = jax.nn.sigmoid(selection)
    weighting = sigma_sel * chosen
    projected = product(sequence, value_full).reshape(row_count, HEADS, ATT_EXPERTS, HEAD_DIM)
    values = jnp.sum(weighting[:, 0, :, :, None] * projected, axis=2).astype(jnp.bfloat16)
    key_full, value_rows = (
        lax.all_gather(key_rows.reshape(row_count, head_width), "dp", axis=0, tiled=True),
        lax.all_gather(values.reshape(row_count, head_width), "dp", axis=0, tiled=True),
    )
    key_heads = key_full.reshape(bucket_rows, HEADS, HEAD_DIM)
    value_heads = value_rows.reshape(bucket_rows, HEADS, HEAD_DIM)
    key_place = jnp.arange(bucket_rows, dtype=jnp.int32)
    allowed = (key_place[None, :] <= query_place[:, None]) & (key_place[None, :] < seq_len)
    scores = (
        jnp.einsum("qhd,khd->hqk", queries, key_heads, preferred_element_type=jnp.float32)
        * score_scale
    )
    scores = jnp.where(allowed[None], scores, masked_score)
    highest = jnp.max(scores, axis=-1, keepdims=True)
    raised = jnp.exp(scores - highest)
    row_total = jnp.sum(raised, axis=-1, keepdims=True)
    log_total = highest + jnp.log(row_total)
    attention_probs = raised / row_total
    attended = jnp.einsum(
        "hqk,khd->qhd",
        attention_probs.astype(jnp.bfloat16),
        value_heads,
        preferred_element_type=jnp.float32,
    )
    mixed_heads = (
        (weighting[:, 1, :, :, None] * attended[:, :, None, :])
        .astype(jnp.bfloat16)
        .reshape(row_count, mixed_width)
    )
    hidden = inputs_f + product_last(mixed_heads, output_full)
    normed_two = layer_norm(hidden, 1.0).astype(jnp.bfloat16)
    logits = product(normed_two, router_full)
    route_gates = jax.nn.sigmoid(jnp.take_along_axis(logits, route_rows, axis=1))
    hot_table = (
        route_rows[:, :, None] == jnp.arange(expert_total, dtype=jnp.int32)[None, None, :]
    ).astype(jnp.int32)
    per_token = jnp.sum(hot_table, axis=1)
    earlier = jnp.cumsum(per_token, axis=0) - per_token
    slots = jnp.take_along_axis(earlier, route_rows, axis=1)
    flat_slots = (place_ids * capacity + slots).reshape(-1)
    counts_local = jnp.sum(per_token * valid[:, None].astype(jnp.int32), axis=0)
    hidden_low = hidden.astype(jnp.bfloat16)
    row_copies = jnp.broadcast_to(hidden_low[:, None, :], (row_count, TOPK, model_width)).reshape(
        -1, model_width
    )
    send_rows = (
        jnp.zeros((expert_total * capacity, model_width), jnp.bfloat16)
        .at[flat_slots]
        .set(row_copies)
    )
    send_rows = send_rows.reshape(-1, share, capacity, model_width)
    received = lax.all_to_all(send_rows, ("dp", "expert"), split_axis=0, concat_axis=0, tiled=True)
    inner = jnp.einsum("necd,edh->nech", received, expert_in, preferred_element_type=jnp.float32)
    active = jax.nn.silu(inner).astype(jnp.bfloat16)
    produced = jnp.einsum(
        "nech,edh->necd", active, expert_out, preferred_element_type=jnp.float32
    ).astype(jnp.bfloat16)
    returned = lax.all_to_all(produced, ("dp", "expert"), split_axis=0, concat_axis=0, tiled=True)
    picked = returned.reshape(expert_total * capacity, model_width)[flat_slots].reshape(
        row_count, TOPK, model_width
    )
    moe_out = jnp.einsum("tk,tkd->td", route_gates, picked, preferred_element_type=jnp.float32)
    layer_out = (hidden + moe_out).astype(jnp.bfloat16)
    upstream = cotangent[0].astype(jnp.float32) * valid[:, None].astype(jnp.float32)
    gate_grad = jnp.einsum("td,tkd->tk", upstream, picked, preferred_element_type=jnp.float32)
    route_slope = gate_grad * route_gates * (1.0 - route_gates)
    grad_copies = (
        (route_gates[:, :, None] * upstream[:, None, :])
        .astype(jnp.bfloat16)
        .reshape(-1, model_width)
    )
    send_grad = (
        jnp.zeros((expert_total * capacity, model_width), jnp.bfloat16)
        .at[flat_slots]
        .set(grad_copies)
    )
    send_grad = send_grad.reshape(-1, share, capacity, model_width)
    grad_in = lax.all_to_all(send_grad, ("dp", "expert"), split_axis=0, concat_axis=0, tiled=True)
    out_grad = jnp.einsum("necd,nech->edh", grad_in, active, preferred_element_type=jnp.float32)
    active_grad = jnp.einsum(
        "necd,edh->nech", grad_in, expert_out, preferred_element_type=jnp.float32
    )
    inner_grad = (active_grad * silu_slope(inner)).astype(jnp.bfloat16)
    in_grad = jnp.einsum("necd,nech->edh", received, inner_grad, preferred_element_type=jnp.float32)
    back_rows = jnp.einsum(
        "nech,edh->necd", inner_grad, expert_in, preferred_element_type=jnp.float32
    ).astype(jnp.bfloat16)
    sent_back = lax.all_to_all(back_rows, ("dp", "expert"), split_axis=0, concat_axis=0, tiled=True)
    moe_input_grad = jnp.sum(
        sent_back.reshape(expert_total * capacity, model_width)[flat_slots]
        .reshape(row_count, TOPK, model_width)
        .astype(jnp.float32),
        axis=1,
    )
    logit_grad = (
        jnp.zeros((row_count, expert_total), jnp.float32)
        .at[jnp.arange(row_count)[:, None], route_rows]
        .set(route_slope)
        .astype(jnp.bfloat16)
    )
    router_grad = product_rows(normed_two, logit_grad)
    normed_two_grad = product_last(logit_grad, router_full)
    hidden_norm_grad = norm_backward(hidden, 1.0, normed_two_grad)[0]
    hidden_grad = upstream + moe_input_grad + hidden_norm_grad
    hidden_grad_low = hidden_grad.astype(jnp.bfloat16)
    output_grad = product_rows(hidden_grad_low, mixed_heads)
    mixed_grad = product(hidden_grad_low, output_full).reshape(
        row_count, HEADS, ATT_EXPERTS, HEAD_DIM
    )
    attended_grad = jnp.sum(weighting[:, 1, :, :, None] * mixed_grad, axis=2)
    out_weighting_grad = jnp.sum(mixed_grad * attended[:, :, None, :], axis=-1)
    attended_low = attended_grad.astype(jnp.bfloat16)
    recomputed = (
        jnp.einsum("qhd,khd->hqk", queries, key_heads, preferred_element_type=jnp.float32)
        * score_scale
    )
    recomputed = jnp.where(allowed[None], recomputed, masked_score)
    probs_again = jnp.exp(recomputed - log_total)
    value_terms = jnp.einsum(
        "hqk,qhd->khd",
        probs_again.astype(jnp.bfloat16),
        attended_low,
        preferred_element_type=jnp.float32,
    )
    prob_grad = jnp.einsum(
        "qhd,khd->hqk", attended_low, value_heads, preferred_element_type=jnp.float32
    )
    delta = jnp.sum(probs_again * prob_grad, axis=-1, keepdims=True)
    score_grad = (probs_again * (prob_grad - delta)).astype(jnp.bfloat16)
    query_grad = (
        jnp.einsum("hqk,khd->qhd", score_grad, key_heads, preferred_element_type=jnp.float32)
        * score_scale
    )
    key_terms = (
        jnp.einsum("hqk,qhd->khd", score_grad, queries, preferred_element_type=jnp.float32)
        * score_scale
    )
    key_grad, value_grad_rows = (
        lax.psum_scatter(
            key_terms.reshape(bucket_rows, head_width), "dp", scatter_dimension=0, tiled=True
        ),
        lax.psum_scatter(
            value_terms.reshape(bucket_rows, head_width), "dp", scatter_dimension=0, tiled=True
        ),
    )
    value_grad_heads = value_grad_rows.reshape(row_count, HEADS, HEAD_DIM)
    projected_grad = (
        (weighting[:, 0, :, :, None] * value_grad_heads[:, :, None, :])
        .astype(jnp.bfloat16)
        .reshape(row_count, mixed_width)
    )
    in_weighting_grad = jnp.sum(value_grad_heads[:, :, None, :] * projected, axis=-1)
    value_grad = product_rows(sequence, projected_grad)
    input_value_grad = product_last(projected_grad, value_full)
    query_back = rotate(query_grad, cosine, sine_table, -1.0)
    key_back = rotate(key_grad.reshape(row_count, HEADS, HEAD_DIM), cosine, sine_table, -1.0)
    query_key_grad = (
        jnp.stack([query_back, key_back], axis=1)
        .astype(jnp.bfloat16)
        .reshape(row_count, 2 * head_width)
    )
    qk_grad = product_rows(normed_low, query_key_grad)
    weighting_grad = jnp.stack([in_weighting_grad, out_weighting_grad], axis=1)
    selection_grad = (
        (weighting_grad * chosen * sigma_sel * (1.0 - sigma_sel))
        .astype(jnp.bfloat16)
        .reshape(row_count, 2 * HEADS * ATT_EXPERTS)
    )
    select_grad = product_rows(normed_low, selection_grad)
    normed_grad = product_last(query_key_grad, qk_full) + product_last(selection_grad, select_full)
    input_norm_grad, gain_grad = norm_backward(inputs_f, gain_one, normed_grad)
    input_grad = hidden_grad + input_value_grad + input_norm_grad
    summed = (
        lax.psum_scatter(qk_grad, ("dp", "expert"), scatter_dimension=0, tiled=True),
        lax.psum_scatter(value_grad, ("dp", "expert"), scatter_dimension=0, tiled=True),
        lax.psum_scatter(output_grad, ("dp", "expert"), scatter_dimension=0, tiled=True),
        lax.psum_scatter(select_grad, ("dp", "expert"), scatter_dimension=0, tiled=True),
        lax.psum_scatter(router_grad, ("dp", "expert"), scatter_dimension=0, tiled=True),
        lax.psum_scatter(gain_grad, ("dp", "expert"), scatter_dimension=0, tiled=True),
    )
    qk_sum, value_sum, output_sum, select_sum, router_sum, gain_sum = summed
    expert_sum = lax.all_to_all(
        jnp.concatenate([in_grad, out_grad], axis=2), "dp", split_axis=1, concat_axis=0, tiled=True
    )
    expert_counts = lax.psum(counts_local, ("dp", "expert"))
    qk_new, qk_first_new, qk_second_new = adamw_update(
        qk_weight, qk_first, qk_second, qk_sum, rate_query_key
    )
    value_new, value_first_new, value_second_new = adamw_update(
        value_weight, value_first, value_second, value_sum, rate_value
    )
    output_new, output_first_new, output_second_new = adamw_update(
        output_weight, output_first, output_second, output_sum, rate_output
    )
    select_new, select_first_new, select_second_new = adamw_update(
        select_weight, select_first, select_second, select_sum, rate_select
    )
    router_new, router_first_new, router_second_new = adamw_update(
        router_weight, router_first, router_second, router_sum, rate_router
    )
    gain_new, gain_first_new, gain_second_new = adamw_update(
        gain_weight, gain_first, gain_second, gain_sum, rate_gain
    )
    expert_new, expert_first_new, expert_second_new = adamw_update(
        expert_weight, expert_first, expert_second, expert_sum, rate_expert
    )
    return (
        layer_out[None],
        input_grad[None],
        qk_new,
        qk_first_new,
        qk_second_new,
        value_new,
        value_first_new,
        value_second_new,
        output_new,
        output_first_new,
        output_second_new,
        select_new,
        select_first_new,
        select_second_new,
        router_new,
        router_first_new,
        router_second_new,
        gain_new,
        gain_first_new,
        gain_second_new,
        expert_new,
        expert_first_new,
        expert_second_new,
        expert_counts,
    )


def solution(mesh):
    placed = (
        P("expert", "dp", None),
        P("expert", "dp", None),
        P("expert"),
        P("expert", "dp", None, None),
        P("expert", "dp", None),
        P(("dp", "expert"), None),
        P(("dp", "expert"), None),
        P(("dp", "expert"), None),
        P(("dp", "expert"), None),
        P(("dp", "expert"), None),
        P(("dp", "expert"), None),
        P(("dp", "expert"), None),
        P(("dp", "expert"), None),
        P(("dp", "expert"), None),
        P(("dp", "expert"), None),
        P(("dp", "expert"), None),
        P(("dp", "expert"), None),
        P(("dp", "expert"), None),
        P(("dp", "expert"), None),
        P(("dp", "expert"), None),
        P(("dp", "expert")),
        P(("dp", "expert")),
        P(("dp", "expert")),
        P("expert", "dp", None),
        P("expert", "dp", None),
        P("expert", "dp", None),
    )
    return jax.shard_map(
        local,
        mesh=mesh,
        in_specs=placed,
        out_specs=(
            P("expert", "dp", None),
            P("expert", "dp", None),
            P(("dp", "expert"), None),
            P(("dp", "expert"), None),
            P(("dp", "expert"), None),
            P(("dp", "expert"), None),
            P(("dp", "expert"), None),
            P(("dp", "expert"), None),
            P(("dp", "expert"), None),
            P(("dp", "expert"), None),
            P(("dp", "expert"), None),
            P(("dp", "expert"), None),
            P(("dp", "expert"), None),
            P(("dp", "expert"), None),
            P(("dp", "expert"), None),
            P(("dp", "expert"), None),
            P(("dp", "expert"), None),
            P(("dp", "expert")),
            P(("dp", "expert")),
            P(("dp", "expert")),
            P("expert", "dp", None),
            P("expert", "dp", None),
            P("expert", "dp", None),
            P(),
        ),
        check_vma=False,
    )
```

profile of v0, /device:TPU:0, one launch (start us, length us, event | category | flops | bytes accessed | tf_op | source)
XLA Modules:
  0.0 2748.6 jit_solution(3535296907969901998)
XLA Ops:
  11.5 42.0 %all-reduce = bf16[1024]{0:T(1024)(128)(2,1)S(1)} all-reduce(bf16[1024]{0:T(1024)(128)(2,1)S(1)} %dynamic-update-slice), channel_id=1, replica_groups=mesh['dp'=4,'expert'=8] {'dp','expert'}, use_global_device_ids=true, to_apply=%add | all-reduce | flops 1024 | bytes 4096
  57.0 13.8 all-gather.10.cloned.1.call-done
  75.8 41.2 %all_gather.25 = bf16[1024,40]{1,0:T(8,128)(2,1)S(1)} all-gather(bf16[32,40]{1,0:T(8,128)(2,1)S(1)} %convert_element_type.200), channel_id=1, replica_groups=mesh['dp'=4,'expert'=8] {'dp','expert'}, dimensions={0}, use_global_device_ids=true | all-gather | bytes 84480 | tf_op jit(solution)/shard_map/all_gather | solution.py:145
  118.9 20.0 all-gather.6.cloned.1.call-done
  164.5 25.6 gather_fusion.3
  210.9 64.0 %all-gather.14.cloned.1.call-done = bf16[1024,2560]{1,0:T(8,128)(2,1)} async-done(((bf16[32,2560]{1,0:T(8,128)(2,1)}), bf16[1024,2560]{1,0:T(8,128)(2,1)}) %all-gather.14.cloned.1.call-update) | async-done | bytes 5242896 | tf_op jit(solution)/shard_map/all_gather | solution.py:144
  284.8 28.0 %scatter_custom_fusion = bf16[7392,1024]{1,0:T(8,128)(2,1)} fusion(s32[4096]{0:T(1024)} %bitcast.280, bf16[4096,1024]{1,0:T(8,128)(2,1)} %bitcast.246, bf16[]{:T(256)} %constant.76.clone.1), kind=kCustom, calls=%fused_computation.18 | custom fusion | bytes 15139328 | tf_op jit(solution)/shard_map/scatter | solution.py:231
  312.7 16.3 reshape.649
  333.2 371.2 %all_gather.31 = bf16[1024,96]{1,0:T(8,128)(2,1)S(1)} all-gather(bf16[32,96]{1,0:T(8,128)(2,1)S(1)} %convert_element_type.214), channel_id=1, replica_groups=mesh['dp'=4,'expert'=8] {'dp','expert'}, dimensions={0}, use_global_device_ids=true | all-gather | bytes 202752 | tf_op jit(solution)/shard_map/all_gather | solution.py:146
  705.8 33.2 %gather_fusion.2 = f32[4096]{0:T(1024)S(1)} fusion(f32[256,96]{0,1:T(8,128)S(1)} %fusion.108, s32[4096]{0:T(1024)S(1)} %reshape.682), kind=kCustom, calls=%fused_computation.2 | custom fusion | bytes 65536 | tf_op jit(solution)/shard_map/jit(take_along_axis)/gather | solution.py:215
  743.0 27.7 %scatter_custom_fusion.1 = bf16[7392,1024]{1,0:T(8,128)(2,1)} fusion(s32[4096]{0:T(1024)} %bitcast.281, bf16[4096,1024]{1,0:T(8,128)(2,1)} %fusion, bf16[]{:T(256)} %constant.76.clone.1), kind=kCustom, calls=%fused_computation.16 | custom fusion | bytes 15139328 | tf_op jit(solution)/shard_map/scatter | solution.py:257
  770.7 16.3 reshape.652
  791.5 11.6 fusion.13
  803.1 330.5 %all-to-all-done.3 = bf16[32,3,77,1024]{3,2,1,0:T(8,128)(2,1)} async-done(((bf16[32,3,77,1024]{3,2,1,0:T(8,128)(2,1)}), bf16[32,3,77,1024]{3,2,1,0:T(8,128)(2,1)}, u32[]{:S(2)}, u32[]{:S(2)}) %all-to-all-start.3) | async-done | bytes 15138848 | tf_op jit(solution)/shard_map/all_to_all | solution.py:260
  1152.8 13.3 copy.222
  1177.9 13.4 copy.219
  1191.3 320.8 %all-to-all-done.4 = bf16[32,3,77,1024]{3,2,1,0:T(8,128)(2,1)} async-done(((bf16[32,3,77,1024]{3,2,1,0:T(8,128)(2,1)}), bf16[32,3,77,1024]{3,2,1,0:T(8,128)(2,1)}, u32[]{:S(2)}, u32[]{:S(2)}) %all-to-all-start.4) | async-done | bytes 15138848 | tf_op jit(solution)/shard_map/all_to_all | solution.py:270
  1516.8 16.5 reshape.653
  1533.3 28.1 %gather_fusion.1 = bf16[4096,1024]{1,0:T(8,128)(2,1)} fusion(bf16[7392,1024]{1,0:T(8,128)(2,1)} %reshape.653, s32[4096]{0:T(1024)S(1)} %broadcast_clamp_fusion), kind=kCustom, calls=%fused_computation.1 | custom fusion | bytes 16793600 | tf_op jit(solution)/shard_map/gather | solution.py:272
  1570.2 288.0 %all-to-all-done.2 = bf16[32,3,77,1024]{3,2,1,0:T(8,128)(2,1)} async-done(((bf16[32,3,77,1024]{3,2,1,0:T(8,128)(2,1)}), bf16[32,3,77,1024]{3,2,1,0:T(8,128)(2,1)}, u32[]{:S(2)}, u32[]{:S(2)}) %all-to-all-start.2) | async-done | bytes 15138848 | tf_op jit(solution)/shard_map/all_to_all | solution.py:240
  1858.2 16.4 reshape.650
  1874.6 28.3 %gather_fusion = bf16[4096,1024]{1,0:T(8,128)(2,1)} fusion(bf16[7392,1024]{1,0:T(8,128)(2,1)} %reshape.650, s32[4096]{0:T(1024)S(1)} %broadcast_clamp_fusion), kind=kCustom, calls=%fused_computation | custom fusion | bytes 16793600 | tf_op jit(solution)/shard_map/gather | solution.py:241
  1914.4 15.6 scatter_custom_fusion.2
  1953.1 20.7 reduce-scatter.12.cloned.1.call-done
  1978.6 34.2 %reduce-scatter.14.cloned.1.call-done = f32[256,512]{0,1:T(8,128)} async-done(((f32[1024,512]{0,1:T(8,128)}), f32[256,512]{0,1:T(8,128)}) %reduce-scatter.14.cloned.1.call-update) | async-done | bytes 524304 | tf_op jit(solution)/shard_map/reduce_scatter | solution.py:321
  2031.1 11.5 copy.254
  2069.2 82.6 %psum.7 = s32[96]{0:T(128)} all-reduce(s32[96]{0:T(128)S(1)} %multiply_reduce_fusion.8), channel_id=1, replica_groups=mesh['dp'=4,'expert'=8] {'dp','expert'}, use_global_device_ids=true, to_apply=%region_33.34 | all-reduce | flops 96 | bytes 768 | tf_op jit(solution)/shard_map/psum | solution.py:367
  2167.4 38.7 %all-reduce.1 = f32[1024]{0:T(1024)S(1)} all-reduce(f32[1024]{0:T(1024)S(1)} %get-tuple-element.122), channel_id=9, replica_groups=mesh['dp'=4,'expert'=8] {'dp','expert'}, use_global_device_ids=true, to_apply=%region_31.32.clone | all-reduce | flops 1024 | bytes 8192
  2212.4 70.8 %reduce-scatter.18.cloned.1.call-done = f32[32,40]{1,0:T(8,128)} async-done(((f32[1024,40]{1,0:T(8,128)}), f32[32,40]{1,0:T(8,128)}) %reduce-scatter.18.cloned.1.call-update) | async-done | bytes 5136 | tf_op jit(solution)/shard_map/reduce_scatter | solution.py:359
  2284.6 139.8 %reduce-scatter.16.cloned.1.call-done = f32[32,1024]{1,0:T(8,128)} async-done(((f32[1024,1024]{1,0:T(8,128)}), f32[32,1024]{1,0:T(8,128)}) %reduce-scatter.16.cloned.1.call-update) | async-done | bytes 131088 | tf_op jit(solution)/shard_map/reduce_scatter | solution.py:356
  2426.2 155.0 %reduce-scatter.24.cloned.1.call-done = f32[32,2560]{1,0:T(8,128)} async-done(((f32[1024,2560]{1,0:T(8,128)}), f32[32,2560]{1,0:T(8,128)}) %reduce-scatter.24.cloned.1.call-update) | async-done | bytes 327696 | tf_op jit(solution)/shard_map/reduce_scatter | solution.py:358
  2583.5 156.0 %reduce-scatter.22.cloned.1.call-done = f32[32,2560]{1,0:T(8,128)} async-done(((f32[1024,2560]{1,0:T(8,128)}), f32[32,2560]{1,0:T(8,128)}) %reduce-scatter.22.cloned.1.call-update) | async-done | bytes 327696 | tf_op jit(solution)/shard_map/reduce_scatter | solution.py:357
  (338 shorter events, 241.2 us)
Async XLA Ops:
  7.2 63.7 %all-gather.10.cloned.1.call-start = ((), (), s32[]{:S(2)}) async-start(), calls=%async_computation.15 | async-start | bytes 2162688 | tf_op jit(solution)/shard_map/all_gather | solution.py:142
  8.8 130.0 %all-gather.6.cloned.1.call-start = ((), (), s32[]{:S(2)}) async-start(), calls=%async_computation.13 | async-start | bytes 5406720 | tf_op jit(solution)/shard_map/all_gather | solution.py:143
  10.6 180.8 %all-gather.12.cloned.1.call-start = ((), (), s32[]{:S(2)}) async-start(), calls=%async_computation.16 | async-start | bytes 1310720 | tf_op jit(solution)/shard_map/all_gather | solution.py:184
  75.7 130.5 %all-gather.8.cloned.1.call-start = ((), (), s32[]{:S(2)}) async-start(), calls=%async_computation.14 | async-start | bytes 1310720 | tf_op jit(solution)/shard_map/all_gather | solution.py:185
  153.3 121.6 %all-gather.14.cloned.1.call-start = ((), (), s32[]{:S(2)}) async-start(), calls=%async_computation.17 | async-start | bytes 5406720 | tf_op jit(solution)/shard_map/all_gather | solution.py:144
  157.3 171.7 %all-to-all-start.1 = ((bf16[12,256,256]{2,1,0:T(8,128)(2,1)}), bf16[12,256,256]{2,1,0:T(8,128)(2,1)S(1)}, u32[]{:S(2)}, u32[]{:S(2)}) async-start(bf16[12,256,256]{2,1,0:T(8,128)(2,1)} %convert_element_type.217), calls=%async_computation.1 | async-start | bytes 3145728 | tf_op jit(solution)/shard_map/all_to_all | solution.py:156
  280.3 425.2 %copy-start.13 = (bf16[256,1024]{1,0:T(8,128)(2,1)}, bf16[256,1024]{1,0:T(8,128)(2,1)S(1)}, u32[]{:S(2)}) copy-start(bf16[256,1024]{1,0:T(8,128)(2,1)S(1)} %get-tuple-element.152) | copy-start | bytes 1572868
  329.0 375.3 %copy-start.11 = (bf16[1,256,1024]{2,1,0:T(8,128)(2,1)S(1)}, bf16[1,256,1024]{2,1,0:T(8,128)(2,1)}, u32[]{:S(2)}) copy-start(bf16[1,256,1024]{2,1,0:T(8,128)(2,1)} %param.27) | copy-start | bytes 1572868
  329.0 458.1 %all-to-all-start = ((bf16[32,3,77,1024]{3,2,1,0:T(8,128)(2,1)}), bf16[32,3,77,1024]{3,2,1,0:T(8,128)(2,1)}, u32[]{:S(2)}, u32[]{:S(2)}) async-start(bf16[32,3,77,1024]{3,2,1,0:T(8,128)(2,1)} %reshape.649), calls=%async_computation | async-start | bytes 31457280 | tf_op jit(solution)/shard_map/all_to_all | solution.py:234
  787.1 346.5 %all-to-all-start.3 = ((bf16[32,3,77,1024]{3,2,1,0:T(8,128)(2,1)}), bf16[32,3,77,1024]{3,2,1,0:T(8,128)(2,1)}, u32[]{:S(2)}, u32[]{:S(2)}) async-start(bf16[32,3,77,1024]{3,2,1,0:T(8,128)(2,1)} %reshape.652), calls=%async_computation.3 | async-start | bytes 31457280 | tf_op jit(solution)/shard_map/all_to_all | solution.py:260
  803.1 366.8 %copy-start.27 = (bf16[32,3,77,128]{3,2,0,1:T(8,128)(2,1)}, bf16[32,3,77,128]{3,2,0,1:T(8,128)(2,1)S(1)}, u32[]{:S(2)}) copy-start(bf16[32,3,77,128]{3,2,0,1:T(8,128)(2,1)S(1)} %get-tuple-element.185) | copy-start | bytes 5677060
  1166.1 346.1 %all-to-all-start.4 = ((bf16[32,3,77,1024]{3,2,1,0:T(8,128)(2,1)}), bf16[32,3,77,1024]{3,2,1,0:T(8,128)(2,1)}, u32[]{:S(2)}, u32[]{:S(2)}) async-start(bf16[32,3,77,1024]{3,2,1,0:T(8,128)(2,1)} %copy.222), calls=%async_computation.4 | async-start | bytes 31457280 | tf_op jit(solution)/shard_map/all_to_all | solution.py:270
  1191.3 324.9 %copy-start.82 = (s32[2]{0:T(128)S(1)}, s32[2]{0:T(128)}, u32[]{:S(2)}) copy-start(s32[2]{0:T(128)} %constant.207) | copy-start | bytes 28
  1191.3 325.2 %copy-start.60 = (s32[4096,1]{0,1:T(1,128)S(1)}, s32[4096,1]{0,1:T(1,128)}, u32[]{:S(2)}) copy-start(s32[4096,1]{0,1:T(1,128)} %compare_select_fusion.1) | copy-start | bytes 49156
  1191.3 325.2 %copy-start.12 = (bf16[1,256,1024]{2,1,0:T(8,128)(2,1)S(1)}, bf16[1,256,1024]{2,1,0:T(8,128)(2,1)}, u32[]{:S(2)}) copy-start(bf16[1,256,1024]{2,1,0:T(8,128)(2,1)} %param.27) | copy-start | bytes 1572868
  1191.3 325.2 %copy-start.75 = (f32[256]{0:T(256)S(1)}, f32[256]{0:T(256)}, u32[]{:S(2)}) copy-start(f32[256]{0:T(256)} %copy-done.74) | copy-start | bytes 3076
  1191.3 325.3 %copy-start.62 = (f32[4,256]{1,0:T(4,128)S(1)}, f32[4,256]{1,0:T(4,128)}, u32[]{:S(2)}) copy-start(f32[4,256]{1,0:T(4,128)} %copy-done.61) | copy-start | bytes 12292
  1191.3 325.3 %copy-start.77 = (f32[4,256]{1,0:T(4,128)S(1)}, f32[4,256]{1,0:T(4,128)}, u32[]{:S(2)}) copy-start(f32[4,256]{1,0:T(4,128)} %copy-done.76) | copy-start | bytes 12292
  1191.3 325.4 %copy-start.30 = (f32[4096]{0:T(1024)S(1)}, f32[4096]{0:T(1024)}, u32[]{:S(2)}) copy-start(f32[4096]{0:T(1024)} %copy-done.29) | copy-start | bytes 49156
  1512.1 346.1 %all-to-all-start.2 = ((bf16[32,3,77,1024]{3,2,1,0:T(8,128)(2,1)}), bf16[32,3,77,1024]{3,2,1,0:T(8,128)(2,1)}, u32[]{:S(2)}, u32[]{:S(2)}) async-start(bf16[32,3,77,1024]{3,2,1,0:T(8,128)(2,1)} %copy.219), calls=%async_computation.2 | async-start | bytes 31457280 | tf_op jit(solution)/shard_map/all_to_all | solution.py:240
  1516.0 457.7 %reduce-scatter.12.cloned.1.call-start = ((), (), s32[]{:S(2)}) async-start(), calls=%async_computation.18 | async-start | bytes 2621440 | tf_op jit(solution)/shard_map/reduce_scatter | solution.py:324
  1940.8 71.9 %reduce-scatter.14.cloned.1.call-start = ((), (), s32[]{:S(2)}) async-start(), calls=%async_computation.19 | async-start | bytes 2621440 | tf_op jit(solution)/shard_map/reduce_scatter | solution.py:321
  1947.4 214.5 %reduce-scatter.20.cloned.1.call-start = ((), (), s32[]{:S(2)}) async-start(), calls=%async_computation.22 | async-start | bytes 540672 | tf_op jit(solution)/shard_map/reduce_scatter | solution.py:360
  1953.0 330.2 %reduce-scatter.18.cloned.1.call-start = ((), (), s32[]{:S(2)}) async-start(), calls=%async_computation.21 | async-start | bytes 540672 | tf_op jit(solution)/shard_map/reduce_scatter | solution.py:359
  1978.5 445.9 %reduce-scatter.16.cloned.1.call-start = ((), (), s32[]{:S(2)}) async-start(), calls=%async_computation.20 | async-start | bytes 4325376 | tf_op jit(solution)/shard_map/reduce_scatter | solution.py:356
  2017.7 563.5 %reduce-scatter.24.cloned.1.call-start = ((), (), s32[]{:S(2)}) async-start(), calls=%async_computation.24 | async-start | bytes 10813440 | tf_op jit(solution)/shard_map/reduce_scatter | solution.py:358
  2024.4 715.0 %reduce-scatter.22.cloned.1.call-start = ((), (), s32[]{:S(2)}) async-start(), calls=%async_computation.23 | async-start | bytes 10813440 | tf_op jit(solution)/shard_map/reduce_scatter | solution.py:357
  2064.1 87.8 %all-to-all-start.5 = ((f32[3,1024,256]{2,0,1:T(4,128)}), f32[3,1024,256]{2,0,1:T(4,128)}, u32[]{:S(2)}, u32[]{:S(2)}) async-start(f32[3,1024,256]{2,0,1:T(4,128)} %copy.236), calls=%async_computation.10 | async-start | bytes 8388608 | tf_op jit(solution)/shard_map/all_to_all | solution.py:364
  2206.7 374.5 %copy-start.34 = (f32[32,2560]{1,0:T(8,128)S(1)}, f32[32,2560]{1,0:T(8,128)}, u32[]{:S(2)}) copy-start(f32[32,2560]{1,0:T(8,128)} %param.37) | copy-start | bytes 983044
  2212.4 527.1 %copy-start.35 = (f32[32,2560]{1,0:T(8,128)S(1)}, f32[32,2560]{1,0:T(8,128)}, u32[]{:S(2)}) copy-start(f32[32,2560]{1,0:T(8,128)} %param.34) | copy-start | bytes 983044
  2212.4 527.1 %copy-start.44 = (f32[32,2560]{1,0:T(8,128)S(1)}, f32[32,2560]{1,0:T(8,128)}, u32[]{:S(2)}) copy-start(f32[32,2560]{1,0:T(8,128)} %param.35) | copy-start | bytes 983044
  2212.4 527.1 %copy-start.45 = (f32[32,2560]{1,0:T(8,128)S(1)}, f32[32,2560]{1,0:T(8,128)}, u32[]{:S(2)}) copy-start(f32[32,2560]{1,0:T(8,128)} %param.36) | copy-start | bytes 983044
  (73 other events, 2546.1 us)
Sparse Core Ops, SparseCore 0:
  11.6 59.2 all-gather.9
  74.3 64.5 all-gather.5
  141.2 35.6 all-gather.11
  179.2 26.9 all-gather.7
  209.5 65.3 all-gather.13
  1941.0 32.7 reduce-scatter.11
  1977.5 35.1 reduce-scatter.13
  2015.0 135.6 reduce-scatter.19
  2153.0 130.2 reduce-scatter.17
  2285.4 138.9 reduce-scatter.15
  2426.7 154.4 reduce-scatter.23
  2583.4 156.0 reduce-scatter.21
where the time goes:
time: 2760 us; the launch traced here: 2750 us
  waiting for transfers between devices  1620 us (59%)
  blocking collectives  576 us (21%)
  local copies, waits for them, and re-layouts  324 us (12%)
  matrix products  126 us (5%)
  other arithmetic  57 us (2%)
    all_gather x1, blocking collectives, local(): lax.all_gather(router_weight.astype(jnp.bfloat16), ('dp', 'expert'), axis...  371 us
    all_to_all x1, waiting for transfers between devices, local(): lax.all_to_all(send_grad, ('dp', 'expert'), split_axis=0, concat_axis=0,...  330 us
    all_to_all x1, waiting for transfers between devices, local(): lax.all_to_all(back_rows, ('dp', 'expert'), split_axis=0, concat_axis=0,...  321 us
    all_to_all x1, waiting for transfers between devices, local(): lax.all_to_all(produced, ('dp', 'expert'), split_axis=0, concat_axis=0, t...  288 us
    reduce_scatter x1, waiting for transfers between devices, local(): lax.psum_scatter(value_grad, ('dp', 'expert'), scatter_dimension=0, tiled...  156 us
    reduce_scatter x1, waiting for transfers between devices, local(): lax.psum_scatter(output_grad, ('dp', 'expert'), scatter_dimension=0, tile...  155 us
    reduce_scatter x1, waiting for transfers between devices, local(): lax.psum_scatter(qk_grad, ('dp', 'expert'), scatter_dimension=0, tiled=True)  140 us
    psum x1, blocking collectives, local(): expert_counts = lax.psum(counts_local, ('dp', 'expert'))  82.6 us
  transfers between devices with their start and end apart: 18, of which 13 were waited for; matrix products, arithmetic and copies ran while one was open for 14% of the time, Pallas kernels for 0%

commit v1 on v0

v1 whole, which is shorter than its diff:
```python
import jax
import jax.numpy as jnp
from jax import lax
from jax.sharding import PartitionSpec as P

HEADS = 4
HEAD_DIM = 128
ATT_EXPERTS = 5
EXPERT_H = 128
TOPK = 16
STEP = 10


norm_eps = 1e-05
beta_first = 0.9
beta_second = 0.95
adam_eps = 1e-08
weight_decay = 0.1
masked_score = -1e30
rope_base = 10000.0
rate_query_key = 0.04
rate_value = 0.03
rate_output = 2.0
rate_select = 0.03
rate_router = 0.015
rate_gain = 1.2
rate_expert = 0.05


def product(former, latter):
    return jnp.dot(former, latter, preferred_element_type=jnp.float32)


def product_rows(former, latter):
    return lax.dot_general(
        former, latter, (((0,), (0,)), ((), ())), preferred_element_type=jnp.float32
    )


def product_last(former, latter):
    return lax.dot_general(
        former, latter, (((1,), (1,)), ((), ())), preferred_element_type=jnp.float32
    )


def layer_norm(values, gain_row):
    center = values - jnp.mean(values, axis=-1, keepdims=True)
    spread = jnp.mean(center * center, axis=-1, keepdims=True)
    return center * lax.rsqrt(spread + norm_eps) * gain_row


def norm_backward(values, gain_row, upstream):
    center = values - jnp.mean(values, axis=-1, keepdims=True)
    inverse = lax.rsqrt(jnp.mean(center * center, axis=-1, keepdims=True) + norm_eps)
    scaled = center * inverse
    gain_grad = jnp.sum(upstream * scaled, axis=0)
    through = upstream * gain_row
    input_grad = inverse * (
        through
        - jnp.mean(through, axis=-1, keepdims=True)
        - scaled * jnp.mean(through * scaled, axis=-1, keepdims=True)
    )
    return (input_grad, gain_grad)


def rope_tables(positions, head_size):
    half_size = head_size // 2
    frequency = jnp.exp(-jnp.log(rope_base) * jnp.arange(half_size).astype(jnp.float32) / half_size)
    angles = positions[:, None] * frequency[None, :]
    return (jnp.cos(angles)[:, None, :], jnp.sin(angles)[:, None, :])


def rotate(head_rows, cosine, sine_table, direction):
    half_size = head_rows.shape[-1] // 2
    leading = head_rows[..., :half_size]
    trailing = head_rows[..., half_size:]
    return jnp.concatenate(
        [
            leading * cosine - direction * trailing * sine_table,
            direction * leading * sine_table + trailing * cosine,
        ],
        axis=-1,
    )


def silu_slope(inner):
    sigma = jax.nn.sigmoid(inner)
    return sigma * (1.0 + inner * (1.0 - sigma))


def adamw_update(weight, first_moment, second_moment, gradient, rate):
    first_new = beta_first * first_moment + (1.0 - beta_first) * gradient
    second_new = beta_second * second_moment + (1.0 - beta_second) * gradient * gradient
    first_hat = first_new / (1.0 - beta_first**STEP)
    second_hat = second_new / (1.0 - beta_second**STEP)
    weight_new = weight - rate * (
        first_hat / (jnp.sqrt(second_hat) + adam_eps) + weight_decay * weight
    )
    return (weight_new, first_new, second_new)


def lower(values):
    return values.astype(jnp.bfloat16)


def swap_dp(values, relative):
    count = lax.axis_size("dp")
    return lax.ppermute(values, "dp", [(place, place ^ relative) for place in range(count)])


def gather_dp(values):
    half = values.shape[0] // 2
    first = swap_dp(values, 1)
    second = swap_dp(values, 2)
    upper = swap_dp(first[:half], 2)
    under = swap_dp(second[half:], 1)
    return [values, first, second, jnp.concatenate([upper, under], axis=0)]


def scatter_dp(parts):
    half = parts[0].shape[0] // 2
    low_parts = [lower(part) for part in parts]
    upper = swap_dp(low_parts[3][:half], 2)
    under = swap_dp(low_parts[3][half:], 1)
    first = lower(
        jnp.concatenate([parts[1][:half] + upper.astype(jnp.float32), parts[1][half:]], axis=0)
    )
    second = lower(
        jnp.concatenate([parts[2][:half], parts[2][half:] + under.astype(jnp.float32)], axis=0)
    )
    return (
        parts[0]
        + swap_dp(first, 1).astype(jnp.float32)
        + swap_dp(second, 2).astype(jnp.float32)
    )


def split_heads(weights, pieces):
    part = weights.shape[0]
    return lower(weights).reshape(part, pieces, HEADS, -1).transpose(2, 0, 1, 3).reshape(HEADS, part, -1)


def local(
    tokens,
    cotangent,
    lengths,
    picks,
    routes,
    qk_weight,
    qk_first,
    qk_second,
    value_weight,
    value_first,
    value_second,
    output_weight,
    output_first,
    output_second,
    select_weight,
    select_first,
    select_second,
    router_weight,
    router_first,
    router_second,
    gain_weight,
    gain_first,
    gain_second,
    expert_weight,
    expert_first,
    expert_second,
):
    row_count = tokens.shape[1]
    model_width = tokens.shape[2]
    group_count = lax.axis_size("dp")
    owner_count = lax.axis_size("expert")
    local_count = expert_weight.shape[0]
    expert_total = local_count * owner_count
    bucket_rows = row_count * group_count
    score_scale = HEAD_DIM ** (-0.5)
    hidden_width = local_count * EXPERT_H
    value_width = ATT_EXPERTS * HEAD_DIM
    part = qk_weight.shape[0]
    select_count = 2 * ATT_EXPERTS
    place = lax.axis_index("dp")
    seq_len = lengths[0]
    sequence = tokens[0]
    route_rows = routes[0]
    own_place = place * row_count + jnp.arange(row_count, dtype=jnp.int32)
    valid = own_place < seq_len

    hot = jnp.max(
        (route_rows[:, :, None] == jnp.arange(expert_total, dtype=jnp.int32)[None, None, :]).astype(
            jnp.float32
        ),
        axis=1,
    )
    counts_local = jnp.sum(hot * valid[:, None].astype(jnp.float32), axis=0)
    count_columns = -(-expert_total // part)
    counts_block = lower(
        jnp.pad(counts_local, (0, count_columns * part - expert_total)).reshape(part, count_columns)
    )

    small_width = select_count + expert_total + 1 + count_columns
    small_pad = -small_width % 128
    shared = jnp.concatenate(
        [
            lower(router_weight),
            lower(gain_weight)[:, None],
            counts_block,
            jnp.zeros((part, small_pad), jnp.bfloat16),
        ],
        axis=1,
    )
    payload = jnp.concatenate(
        [
            split_heads(qk_weight, 2),
            split_heads(value_weight, 1),
            split_heads(output_weight, 1),
            split_heads(select_weight, 2),
            jnp.broadcast_to(shared[None], (HEADS,) + shared.shape),
        ],
        axis=2,
    )
    mine = lax.all_to_all(payload, "dp", split_axis=0, concat_axis=0, tiled=True)
    dense = lax.all_gather(mine, "expert", axis=1, tiled=True).reshape(model_width, -1)
    edge = 2 * HEAD_DIM
    qk_head = dense[:, :edge]
    value_head = dense[:, edge : edge + value_width]
    output_head = dense[:, edge + value_width : edge + 2 * value_width]
    edge = edge + 2 * value_width
    select_head = dense[:, edge : edge + select_count]
    edge = edge + select_count
    router_full = dense[:, edge : edge + expert_total]
    edge = edge + expert_total
    gain_one = dense[:, edge].astype(jnp.float32)
    edge = edge + 1
    expert_counts = jnp.sum(
        dense[:, edge : edge + count_columns]
        .reshape(group_count * owner_count, part * count_columns)[:, :expert_total]
        .astype(jnp.float32),
        axis=0,
    ).astype(jnp.int32)

    expert_low = lower(expert_weight)
    expert_rows = jnp.concatenate(
        [
            expert_low[:, :, :EXPERT_H].transpose(1, 0, 2).reshape(row_count, hidden_width),
            expert_low[:, :, EXPERT_H:].transpose(1, 0, 2).reshape(row_count, hidden_width),
        ],
        axis=1,
    )
    expert_full = lax.all_gather(expert_rows, "dp", axis=0, tiled=True)
    expert_in = expert_full[:, :hidden_width]
    expert_out = expert_full[:, hidden_width:]

    chosen_own = jnp.sum(
        (picks[0][..., None] == jnp.arange(ATT_EXPERTS, dtype=jnp.int32)).astype(jnp.float32),
        axis=-2,
    )
    chosen_own = (
        chosen_own.reshape(row_count, 2, HEADS, ATT_EXPERTS)
        .transpose(0, 2, 1, 3)
        .reshape(row_count, HEADS * select_count)
    )
    chosen_own = jnp.pad(lower(chosen_own), ((0, 0), (0, -(HEADS * select_count) % 128)))
    token_blocks = gather_dp(jnp.concatenate([sequence, chosen_own], axis=1))
    token_rows = jnp.concatenate(token_blocks, axis=0)
    inputs_low = token_rows[:, :model_width]
    inputs_f = inputs_low.astype(jnp.float32)
    chosen = lax.dynamic_slice_in_dim(
        token_rows[:, model_width:], place * select_count, select_count, axis=1
    ).astype(jnp.float32)
    positions = jnp.concatenate(
        [
            (place ^ relative) * row_count + jnp.arange(row_count, dtype=jnp.int32)
            for relative in range(group_count)
        ]
    )
    cosine, sine_table = rope_tables(positions.astype(jnp.float32), HEAD_DIM)
    cosine, sine_table = cosine[:, 0], sine_table[:, 0]

    normed_low = lower(layer_norm(inputs_f, gain_one))
    query_key = product(normed_low, qk_head)
    queries = lower(rotate(query_key[:, :HEAD_DIM], cosine, sine_table, 1.0))
    key_rows = lower(rotate(query_key[:, HEAD_DIM:], cosine, sine_table, 1.0))
    sigma_sel = jax.nn.sigmoid(product(normed_low, select_head))
    weighting = sigma_sel * chosen
    projected = product(inputs_low, value_head).reshape(bucket_rows, ATT_EXPERTS, HEAD_DIM)
    weight_in = weighting[:, :ATT_EXPERTS, None]
    weight_out = weighting[:, ATT_EXPERTS:, None]
    values = lower(jnp.sum(weight_in * projected, axis=1))
    allowed = (positions[None, :] <= positions[:, None]) & (positions[None, :] < seq_len)
    scores = jnp.where(allowed, product_last(queries, key_rows) * score_scale, masked_score)
    highest = jnp.max(scores, axis=-1, keepdims=True)
    raised = jnp.exp(scores - highest)
    attention_probs = raised / jnp.sum(raised, axis=-1, keepdims=True)
    probs_low = lower(attention_probs)
    attended = product(probs_low, values)
    mixed = lower(weight_out * attended[:, None, :]).reshape(bucket_rows, value_width)
    branch = product_last(mixed, output_head).reshape(group_count, row_count, model_width)
    hidden = sequence.astype(jnp.float32) + scatter_dp([branch[r] for r in range(group_count)])

    normed_two = lower(layer_norm(hidden, 1.0))
    gate_table = jax.nn.sigmoid(product(normed_two, router_full)) * hot
    gates = lax.all_to_all(
        gate_table.T.reshape(owner_count, local_count, row_count),
        "expert",
        split_axis=0,
        concat_axis=0,
        tiled=True,
    )
    gates = gates.transpose(0, 2, 1).reshape(owner_count * row_count, local_count)
    wide = (owner_count * row_count, local_count, EXPERT_H)
    gates_wide = jnp.broadcast_to(gates[:, :, None], wide).reshape(-1, hidden_width)
    expert_rows_in = lax.all_gather(lower(hidden), "expert", axis=0, tiled=True)
    upstream_low = jnp.where(valid[:, None], cotangent[0], jnp.zeros((), jnp.bfloat16))
    upstream = upstream_low.astype(jnp.float32)
    expert_up = lax.all_gather(upstream_low, "expert", axis=0, tiled=True)

    inner = product(expert_rows_in, expert_in)
    sigma = jax.nn.sigmoid(inner)
    active = lower(inner * sigma).astype(jnp.float32)
    gated = lower(gates_wide * active)
    produced = product_last(gated, expert_out)
    moe_out = lax.psum_scatter(
        lower(produced), "expert", scatter_dimension=0, tiled=True
    ).astype(jnp.float32)
    layer_out = lower(hidden + moe_out)
    out_terms = product(expert_up, expert_out)
    gate_terms = jnp.sum((out_terms * active).reshape(wide), axis=-1)
    inner_grad = lower(gates_wide * out_terms * sigma * (1.0 + inner * (1.0 - sigma)))
    back = product_last(inner_grad, expert_in)
    moe_input_grad = lax.psum_scatter(
        lower(back), "expert", scatter_dimension=0, tiled=True
    ).astype(jnp.float32)
    gate_grad = lax.all_to_all(
        gate_terms.reshape(owner_count, row_count, local_count).transpose(0, 2, 1),
        "expert",
        split_axis=0,
        concat_axis=0,
        tiled=True,
    )
    gate_grad = gate_grad.reshape(expert_total, row_count).T
    expert_grad = jnp.concatenate(
        [product_rows(expert_rows_in, inner_grad), product_rows(expert_up, gated)], axis=1
    )
    expert_sum = lax.psum_scatter(
        lower(expert_grad), "dp", scatter_dimension=0, tiled=True
    ).astype(jnp.float32)
    expert_sum = (
        expert_sum.reshape(row_count, 2, local_count, EXPERT_H)
        .transpose(2, 0, 1, 3)
        .reshape(local_count, row_count, 2 * EXPERT_H)
    )

    logit_grad = lower(gate_grad * gate_table * (1.0 - gate_table))
    router_grad = product_rows(normed_two, logit_grad)
    normed_two_grad = product_last(logit_grad, router_full)
    hidden_norm_grad = norm_backward(hidden, 1.0, normed_two_grad)[0]
    hidden_grad = upstream + moe_input_grad + hidden_norm_grad
    hidden_grad_low = jnp.concatenate(gather_dp(lower(hidden_grad)), axis=0)

    output_grad = product_rows(hidden_grad_low, mixed)
    mixed_grad = product(hidden_grad_low, output_head).reshape(bucket_rows, ATT_EXPERTS, HEAD_DIM)
    attended_low = lower(jnp.sum(weight_out * mixed_grad, axis=1))
    out_weighting_grad = jnp.sum(mixed_grad * attended[:, None, :], axis=-1)
    value_terms = product_rows(probs_low, attended_low)
    prob_grad = product_last(attended_low, values)
    delta = jnp.sum(attention_probs * prob_grad, axis=-1, keepdims=True)
    score_grad = lower(attention_probs * (prob_grad - delta))
    query_grad = product(score_grad, key_rows) * score_scale
    key_grad = product_rows(score_grad, queries) * score_scale
    projected_grad = lower(weight_in * value_terms[:, None, :]).reshape(bucket_rows, value_width)
    in_weighting_grad = jnp.sum(value_terms[:, None, :] * projected, axis=-1)
    value_grad = product_rows(inputs_low, projected_grad)
    query_key_grad = lower(
        jnp.concatenate(
            [
                rotate(query_grad, cosine, sine_table, -1.0),
                rotate(key_grad, cosine, sine_table, -1.0),
            ],
            axis=1,
        )
    )
    qk_grad = product_rows(normed_low, query_key_grad)
    weighting_grad = jnp.concatenate([in_weighting_grad, out_weighting_grad], axis=1)
    selection_grad = lower(weighting_grad * chosen * sigma_sel * (1.0 - sigma_sel))
    select_grad = product_rows(normed_low, selection_grad)
    normed_grad = product_last(query_key_grad, qk_head) + product_last(selection_grad, select_head)
    input_norm_grad, gain_grad = norm_backward(inputs_f, gain_one, normed_grad)
    input_terms = (product_last(projected_grad, value_head) + input_norm_grad).reshape(
        group_count, row_count, model_width
    )
    input_grad = hidden_grad + scatter_dp([input_terms[r] for r in range(group_count)])

    dense_grad = lower(
        jnp.concatenate(
            [
                qk_grad,
                value_grad,
                output_grad,
                select_grad,
                router_grad,
                gain_grad[:, None],
                jnp.zeros((model_width, small_pad + count_columns), jnp.float32),
            ],
            axis=1,
        )
    )
    dense_grad = dense_grad.reshape(group_count, owner_count, part, -1).transpose(1, 0, 2, 3)
    dense_sum = lax.psum_scatter(dense_grad, "expert", scatter_dimension=0, tiled=True)[0]
    dense_sum = lax.all_to_all(dense_sum, "dp", split_axis=0, concat_axis=0, tiled=True).astype(
        jnp.float32
    )

    def join_heads(columns, pieces):
        return columns.reshape(HEADS, part, pieces, -1).transpose(1, 2, 0, 3).reshape(part, -1)

    edge = 2 * HEAD_DIM
    qk_sum = join_heads(dense_sum[:, :, :edge], 2)
    value_sum = join_heads(dense_sum[:, :, edge : edge + value_width], 1)
    output_sum = join_heads(dense_sum[:, :, edge + value_width : edge + 2 * value_width], 1)
    edge = edge + 2 * value_width
    select_sum = join_heads(dense_sum[:, :, edge : edge + select_count], 2)
    edge = edge + select_count
    shared_sum = jnp.sum(dense_sum[:, :, edge : edge + expert_total + 1], axis=0)
    router_sum = shared_sum[:, :expert_total]
    gain_sum = shared_sum[:, expert_total]
    qk_new, qk_first_new, qk_second_new = adamw_update(
        qk_weight, qk_first, qk_second, qk_sum, rate_query_key
    )
    value_new, value_first_new, value_second_new = adamw_update(
        value_weight, value_first, value_second, value_sum, rate_value
    )
    output_new, output_first_new, output_second_new = adamw_update(
        output_weight, output_first, output_second, output_sum, rate_output
    )
    select_new, select_first_new, select_second_new = adamw_update(
        select_weight, select_first, select_second, select_sum, rate_select
    )
    router_new, router_first_new, router_second_new = adamw_update(
        router_weight, router_first, router_second, router_sum, rate_router
    )
    gain_new, gain_first_new, gain_second_new = adamw_update(
        gain_weight, gain_first, gain_second, gain_sum, rate_gain
    )
    expert_new, expert_first_new, expert_second_new = adamw_update(
        expert_weight, expert_first, expert_second, expert_sum, rate_expert
    )
    return (
        layer_out[None],
        input_grad[None],
        qk_new,
        qk_first_new,
        qk_second_new,
        value_new,
        value_first_new,
        value_second_new,
        output_new,
        output_first_new,
        output_second_new,
        select_new,
        select_first_new,
        select_second_new,
        router_new,
        router_first_new,
        router_second_new,
        gain_new,
        gain_first_new,
        gain_second_new,
        expert_new,
        expert_first_new,
        expert_second_new,
        expert_counts,
    )


def solution(mesh):
    placed = (
        P("expert", "dp", None),
        P("expert", "dp", None),
        P("expert"),
        P("expert", "dp", None, None),
        P("expert", "dp", None),
        P(("dp", "expert"), None),
        P(("dp", "expert"), None),
        P(("dp", "expert"), None),
        P(("dp", "expert"), None),
        P(("dp", "expert"), None),
        P(("dp", "expert"), None),
        P(("dp", "expert"), None),
        P(("dp", "expert"), None),
        P(("dp", "expert"), None),
        P(("dp", "expert"), None),
        P(("dp", "expert"), None),
        P(("dp", "expert"), None),
        P(("dp", "expert"), None),
        P(("dp", "expert"), None),
        P(("dp", "expert"), None),
        P(("dp", "expert")),
        P(("dp", "expert")),
        P(("dp", "expert")),
        P("expert", "dp", None),
        P("expert", "dp", None),
        P("expert", "dp", None),
    )
    return jax.shard_map(
        local,
        mesh=mesh,
        in_specs=placed,
        out_specs=(
            P("expert", "dp", None),
            P("expert", "dp", None),
            P(("dp", "expert"), None),
            P(("dp", "expert"), None),
            P(("dp", "expert"), None),
            P(("dp", "expert"), None),
            P(("dp", "expert"), None),
            P(("dp", "expert"), None),
            P(("dp", "expert"), None),
            P(("dp", "expert"), None),
            P(("dp", "expert"), None),
            P(("dp", "expert"), None),
            P(("dp", "expert"), None),
            P(("dp", "expert"), None),
            P(("dp", "expert"), None),
            P(("dp", "expert"), None),
            P(("dp", "expert"), None),
            P(("dp", "expert")),
            P(("dp", "expert")),
            P(("dp", "expert")),
            P("expert", "dp", None),
            P("expert", "dp", None),
            P("expert", "dp", None),
            P(),
        ),
        check_vma=False,
    )
```

time: 2760 us -> 628 us (0.23)
  waiting for transfers between devices: 1620 us -> 295 us
  blocking collectives: 576 us -> 22.4 us
  local copies, waits for them, and re-layouts: 324 us -> 75.7 us
    all_to_all x6 -> x2, waiting for transfers between devices: 939 us -> 11.9 us  [the longest x1 6.55 us: local(): lax.all_to_all(dense_sum, 'dp', split_axis=0, concat_axis=0, tiled=True)]
    reduce_scatter x7 -> x3, waiting for transfers between devices: 576 us -> 104 us  [the longest x1 48 us: local(): lax.psum_scatter(lower(back), 'expert', scatter_dimension=0, tiled=True)]
    all_gather x2 -> x0, blocking collectives: 412 us -> none  [the longest x1 371 us: local(): lax.all_gather(router_weight.astype(jnp.bfloat16), ('dp', 'expert'), axis...]
    gather x8 -> x0, local copies, waits for them, and re-layouts: 116 us -> none  [the longest x5 33.5 us: local(): jnp.take_along_axis(logits, route_rows, axis=1)]
    psum x1 -> x0, blocking collectives: 82.6 us -> none  [local(): expert_counts = lax.psum(counts_local, ('dp', 'expert'))]
    dot_general x14 -> x0, matrix products: 81.1 us -> none  [the longest x1 11.6 us: local(): jnp.einsum('necd,edh->nech', received, expert_in, preferred_element_type=...]
    unnamed x2 -> x0, blocking collectives: 80.7 us -> none
    reshape x5 -> x14, local copies, waits for them, and re-layouts: 65.5 us -> 3.98 us  [the longest x2 1.91 us: local(): expert_sum = expert_sum.reshape(row_count, 2, local_count, EXPERT_H).tran...]
  transfers between devices with their start and end apart: 18 -> 26, of which waited for: 13 -> 18; matrix products, arithmetic and copies ran while one was open for 14% -> 24% of each run, Pallas kernels for 0% -> 1%
where the time goes in v1:
time: 628 us; the launch traced here: 619 us
  waiting for transfers between devices  295 us (47%)
  matrix products  121 us (19%)
  local copies, waits for them, and re-layouts  75.7 us (12%)
  other arithmetic  59.9 us (10%)
  starting transfers between devices  24.3 us (4%)
  blocking collectives  22.4 us (4%)
  between operations  16.6 us (3%)
    all_gather x1, waiting for transfers between devices, local(): expert_full = lax.all_gather(expert_rows, 'dp', axis=0, tiled=True)  53.1 us
    reduce_scatter x1, waiting for transfers between devices, local(): lax.psum_scatter(lower(back), 'expert', scatter_dimension=0, tiled=True)  48 us
    reduce_scatter x1, waiting for transfers between devices, local(): lax.psum_scatter(lower(expert_grad), 'dp', scatter_dimension=0, tiled=True)  44.8 us
    dot_general x8, matrix products, product(): return jnp.dot(former, latter, preferred_element_type=jnp.float32)  44.4 us
    dot_general x9, matrix products, product_last(): lax.dot_general(former, latter, (((1,), (1,)), ((), ())), preferred_eleme...  44.2 us
    unnamed x159, local copies, waits for them, and re-layouts  43 us
    unnamed x9, waiting for transfers between devices  41.1 us
    ppermute x16, waiting for transfers between devices, swap_dp(): lax.ppermute(values, 'dp', [(place, place ^ relative) for place in range(...  39.8 us
  transfers between devices with their start and end apart: 26, of which 18 were waited for; matrix products, arithmetic and copies ran while one was open for 24% of the time, Pallas kernels for 1%

profile of v1, /device:TPU:0, one launch (start us, length us, event | category | flops | bytes accessed | tf_op | source)
XLA Modules:
  0.0 619.4 jit_solution(2879126062443043677)
XLA Ops:
  15.4 12.7 %all_to_all.20 = bf16[4,32,1664]{2,1,0:T(8,128)(2,1)S(1)} all-to-all(bf16[4,32,1664]{2,1,0:T(8,128)(2,1)S(1)} %copy.256), channel_id=1, replica_groups=mesh['dp'=4,'expert'=8] {'dp'}, dimensions={0} | all-to-all | bytes 851968 | tf_op jit(solution)/shard_map/all_to_all | solution.py:223
  38.4 12.8 %collective-permute-done = bf16[256,1152]{0,1:T(8,128)(2,1)} collective-permute-done((bf16[256,1152]{0,1:T(8,128)(2,1)}, bf16[256,1152]{0,1:T(8,128)(2,1)}, u32[]{:S(2)}, u32[]{:S(2)}) %collective-permute-start) | collective-permute-done | bytes 589856 | tf_op jit(solution)/shard_map/ppermute | solution.py:108
  61.9 7.2 %all-gather.5.cloned.1.call-done = bf16[4,256,1664]{2,0,1:T(4,128)(2,1)} async-done(((bf16[4,32,1664]{2,0,1:T(4,128)(2,1)}), bf16[4,256,1664]{2,0,1:T(4,128)(2,1)}) %all-gather.5.cloned.1.call-update) | async-done | bytes 3407888 | tf_op jit(solution)/shard_map/all_gather | solution.py:224
  83.5 3.8 fusion.139
  87.4 4.5 online-softmax
  100.3 5.5 collective-permute-done.4
  109.4 10.9 %collective-permute-done.7 = bf16[256,1024]{0,1:T(8,128)(2,1)S(1)} collective-permute-done((bf16[256,1024]{0,1:T(8,128)(2,1)S(1)}, bf16[256,1024]{0,1:T(8,128)(2,1)S(1)}, u32[]{:S(2)}, u32[]{:S(2)}) %collective-permute-start.7) | collective-permute-done | bytes 524320 | tf_op jit(solution)/shard_map/ppermute | solution.py:108
  125.2 9.7 %all_to_all.21 = f32[8,12,256]{2,1,0:T(8,128)S(1)} all-to-all(f32[8,12,256]{2,1,0:T(8,128)S(1)} %reshape.342), channel_id=1, replica_groups=mesh['dp'=4,'expert'=8] {'expert'}, dimensions={0} | all-to-all | bytes 196608 | tf_op jit(solution)/shard_map/all_to_all | solution.py:304
  135.0 53.1 %all-gather.9.cloned.1.call-done = bf16[1024,3072]{0,1:T(8,128)(2,1)} async-done(((bf16[256,3072]{0,1:T(8,128)(2,1)}), bf16[1024,3072]{0,1:T(8,128)(2,1)}) %all-gather.9.cloned.1.call-update) | async-done | bytes 6291472 | tf_op jit(solution)/shard_map/all_gather | solution.py:251
  188.1 12.2 %fusion.21 = f32[2048,1536]{0,1:T(8,128)} fusion(bf16[2048,1024]{0,1:T(8,128)(2,1)} %all-gather.11.cloned.1.call-done, bf16[1024,3072]{0,1:T(8,128)(2,1)} %all-gather.9.cloned.1.call-done), kind=kOutput, calls=%fused_computation.41 | convolution fusion | flops 6442450944 | bytes 19922944 | tf_op jit(solution)/shard_map/dot_general | solution.py:31
  200.3 37.7 %all-gather.7.cloned.1.call-done = bf16[2048,1024]{0,1:T(8,128)(2,1)} async-done(((bf16[256,1024]{0,1:T(8,128)(2,1)}), bf16[2048,1024]{0,1:T(8,128)(2,1)}) %all-gather.7.cloned.1.call-update) | async-done | bytes 4194320 | tf_op jit(solution)/shard_map/all_gather | solution.py:314
  238.0 20.9 %fusion.3 = (bf16[2048,1536]{0,1:T(8,128)(2,1)}, f32[2048,1536]{0,1:T(8,128)}, bf16[2048,1536]{0,1:T(8,128)(2,1)}) fusion(f32[2048,1536]{0,1:T(8,128)} %fusion.21, f32[2048,12]{0,1:T(8,128)S(1)} %bitcast.200, bf16[2048,1024]{0,1:T(8,128)(2,1)} %all-gather.7.cloned.1.call-done, bf16[1024,3072]{0,1:T(8,128)(2,1)} %all-gather.9.cloned.1.call-done), kind=kOutput, calls=%fused_computation.6 | convolution fusion | flops 6492782592 | bytes 45187072 | tf_op jit(solution)/shard_map/dot_general | solution.py:31
  258.9 11.6 %convolution_convert_fusion.3 = bf16[2048,1024]{0,1:T(8,128)(2,1)} fusion(bf16[2048,1536]{0,1:T(8,128)(2,1)} %get-tuple-element.179, bf16[1024,3072]{0,1:T(8,128)(2,1)} %all-gather.9.cloned.1.call-done), kind=kOutput, calls=%fused_computation.33 | convolution fusion | flops 6444548096 | bytes 13631488 | tf_op jit(solution)/shard_map/dot_general | solution.py:41
  270.6 12.1 %convolution_convert_fusion.2 = bf16[2048,1024]{0,1:T(8,128)(2,1)} fusion(bf16[2048,1536]{0,1:T(8,128)(2,1)} %get-tuple-element.177, bf16[1024,3072]{0,1:T(8,128)(2,1)} %all-gather.9.cloned.1.call-done), kind=kOutput, calls=%fused_computation.32 | convolution fusion | flops 6444548096 | bytes 13631488 | tf_op jit(solution)/shard_map/dot_general | solution.py:41
  284.2 6.0 reduce_sum.204
  294.4 3.7 fusion.18
  298.1 5.4 all-to-all-done.2
  310.0 11.0 %reduce-scatter.7.cloned.1.call-done = bf16[256,1024]{0,1:T(8,128)(2,1)} async-done(((bf16[2048,1024]{0,1:T(8,128)(2,1)}), bf16[256,1024]{0,1:T(8,128)(2,1)}) %reduce-scatter.7.cloned.1.call-update) | async-done | bytes 524304 | tf_op jit(solution)/shard_map/reduce_scatter | solution.py:324
  323.4 48.0 %reduce-scatter.9.cloned.1.call-done = bf16[256,1024]{0,1:T(8,128)(2,1)} async-done(((bf16[2048,1024]{0,1:T(8,128)(2,1)}), bf16[256,1024]{0,1:T(8,128)(2,1)}) %reduce-scatter.9.cloned.1.call-update) | async-done | bytes 524304 | tf_op jit(solution)/shard_map/reduce_scatter | solution.py:332
  377.7 10.1 %convolution_convert_fusion = bf16[1024,1536]{1,0:T(8,128)(2,1)} fusion(bf16[2048,1024]{0,1:T(8,128)(2,1)S(1)} %copy-done.63, bf16[2048,1536]{0,1:T(8,128)(2,1)} %get-tuple-element.179), kind=kOutput, calls=%fused_computation.30 | convolution fusion | flops 6444023808 | bytes 13631488 | tf_op jit(solution)/shard_map/dot_general | solution.py:35
  421.6 5.0 convolution_convert_fusion.5
  429.6 6.6 %concatenate.96 = bf16[4,8,32,1664]{3,2,1,0:T(8,128)(2,1)} concatenate(bf16[4,8,32,256]{3,2,1,0:T(8,128)(2,1)} %bitcast.205, bf16[4,8,32,640]{3,2,1,0:T(8,128)(2,1)} %convolution_convert_fusion.5, bf16[4,8,32,640]{3,2,1,0:T(8,128)(2,1)} %convolution_convert_fusion.4, bf16[4,8,32,10]{3,2,1,0:T(8,128)(2,1)S(1)} %bitcast.197, bf16[4,8,32,96]{3,2,1,0:T(8,128)(2,1)S(1)} %bitcast.196, ...), dimensions={3} | concatenate | bytes 6815744 | tf_op jit(solution)/shard_map/concatenate | solution.py:396
  436.2 10.2 %convolution_convert_fusion.1 = bf16[1024,1536]{1,0:T(8,128)(2,1)S(1)} fusion(bf16[2048,1024]{0,1:T(8,128)(2,1)} %all-gather.7.cloned.1.call-done, bf16[2048,1536]{0,1:T(8,128)(2,1)} %get-tuple-element.177), kind=kOutput, calls=%fused_computation.31 | convolution fusion | flops 6444023808 | bytes 13631488 | tf_op jit(solution)/shard_map/dot_general | solution.py:35
  446.5 3.6 pad_maximum_fusion
  450.2 5.5 fusion.140
  458.4 3.9 collective-permute-done.12
  470.4 3.6 copy.297
  477.5 40.9 %all-reduce.4.cloned.1.call-done = bf16[8,4,32,1664]{3,2,0,1:T(8,128)(2,1)} async-done(((bf16[8,4,32,1664]{3,2,0,1:T(8,128)(2,1)}), bf16[8,4,32,1664]{3,2,0,1:T(8,128)(2,1)}) %all-reduce.4.cloned.1.call-update) | async-done | bytes 3407888
  520.9 3.9 all-to-all-start.3
  527.8 6.6 %all-to-all-done.3 = bf16[4,32,1664]{2,1,0:T(8,128)(2,1)S(1)} async-done(((bf16[4,32,1664]{2,1,0:T(8,128)(2,1)}), bf16[4,32,1664]{2,1,0:T(8,128)(2,1)S(1)}, u32[]{:S(2)}, u32[]{:S(2)}) %all-to-all-start.3) | async-done | bytes 426016 | tf_op jit(solution)/shard_map/all_to_all | solution.py:411
  547.8 44.8 %reduce-scatter.11.cloned.1.call-done = bf16[256,3072]{1,0:T(8,128)(2,1)} async-done(((bf16[1024,3072]{1,0:T(8,128)(2,1)}), bf16[256,3072]{1,0:T(8,128)(2,1)}) %reduce-scatter.11.cloned.1.call-update) | async-done | bytes 1572880 | tf_op jit(solution)/shard_map/reduce_scatter | solution.py:346
  597.1 5.5 multiply_subtract_fusion
  (346 shorter events, 163.7 us)
Async XLA Ops:
  7.2 62.0 %all-gather.5.cloned.1.call-start = ((), (), s32[]{:S(2)}) async-start(), calls=%async_computation.7 | async-start | bytes 3833856 | tf_op jit(solution)/shard_map/all_gather | solution.py:224
  9.1 20.1 %copy-start.36 = (bf16[1,256,1024]{2,1,0:T(8,128)(2,1)S(1)}, bf16[1,256,1024]{2,1,0:T(8,128)(2,1)}, u32[]{:S(2)}) copy-start(bf16[1,256,1024]{2,1,0:T(8,128)(2,1)} %param.27) | copy-start | bytes 1572868
  29.1 105.9 %all-gather.11.cloned.1.call-start = ((), (), s32[]{:S(2)}) async-start(), calls=%async_computation.11 | async-start | bytes 4718592 | tf_op jit(solution)/shard_map/all_gather | solution.py:317
  30.4 157.8 %all-gather.9.cloned.1.call-start = ((), (), s32[]{:S(2)}) async-start(), calls=%async_computation.9 | async-start | bytes 7864320 | tf_op jit(solution)/shard_map/all_gather | solution.py:251
  35.7 202.3 %all-gather.7.cloned.1.call-start = ((), (), s32[]{:S(2)}) async-start(), calls=%async_computation.8 | async-start | bytes 4718592 | tf_op jit(solution)/shard_map/all_gather | solution.py:314
  36.1 24.8 %copy-start.15 = (bf16[1,256,1024]{1,2,0:T(8,128)(2,1)}, bf16[1,256,1024]{1,2,0:T(8,128)(2,1)S(1)}, u32[]{:S(2)}) copy-start(bf16[1,256,1024]{1,2,0:T(8,128)(2,1)S(1)} %copy.248) | copy-start | bytes 1572868
  37.1 14.1 %collective-permute-start = (bf16[256,1152]{0,1:T(8,128)(2,1)}, bf16[256,1152]{0,1:T(8,128)(2,1)}, u32[]{:S(2)}, u32[]{:S(2)}) collective-permute-start(bf16[256,1152]{0,1:T(8,128)(2,1)} %get-tuple-element.202), channel_id=1, source_target_pairs={{0,8},{8,0},{16,24},{24,16},{1,9},{9,1},{17,25},{25,17},{2,10},{10... | collective-permute-start | bytes 1769480 | tf_op jit(solution)/shard_map/ppermute | solution.py:108
  37.7 15.2 %collective-permute-start.1 = (bf16[256,1152]{0,1:T(8,128)(2,1)}, bf16[256,1152]{0,1:T(8,128)(2,1)}, u32[]{:S(2)}, u32[]{:S(2)}) collective-permute-start(bf16[256,1152]{0,1:T(8,128)(2,1)} %get-tuple-element.202), channel_id=1, source_target_pairs={{0,16},{8,24},{16,0},{24,8},{1,17},{9,25},{17,1},{25,9},{2,18},{10... | collective-permute-start | bytes 1769480 | tf_op jit(solution)/shard_map/ppermute | solution.py:108
  38.3 43.7 %copy-start.59 = (f32[64]{0:T(128)}, f32[64]{0:T(128)S(1)}, u32[]{:S(2)}) copy-start(f32[64]{0:T(128)S(1)} %multiply_exponential_fusion) | copy-start | bytes 772
  52.2 6.8 %collective-permute-start.2 = (bf16[128,1152]{0,1:T(8,128)(2,1)S(1)}, bf16[128,1152]{0,1:T(8,128)(2,1)S(1)}, u32[]{:S(2)}, u32[]{:S(2)}) collective-permute-start(bf16[128,1152]{0,1:T(8,128)(2,1)S(1)} %slice.235), channel_id=1, source_target_pairs={{0,16},{8,24},{16,0},{24,8},{1,17},{9,25},{17,1},{25,9},{2,18},{10... | collective-permute-start | bytes 884744 | tf_op jit(solution)/shard_map/ppermute | solution.py:108
  54.0 6.8 %collective-permute-start.3 = (bf16[128,1152]{0,1:T(8,128)(2,1)S(1)}, bf16[128,1152]{0,1:T(8,128)(2,1)S(1)}, u32[]{:S(2)}, u32[]{:S(2)}) collective-permute-start(bf16[128,1152]{0,1:T(8,128)(2,1)S(1)} %slice.236), channel_id=1, source_target_pairs={{0,8},{8,0},{16,24},{24,16},{1,9},{9,1},{17,25},{25,17},{2,10},{10... | collective-permute-start | bytes 884744 | tf_op jit(solution)/shard_map/ppermute | solution.py:108
  97.1 23.7 %copy-start.16 = (bf16[1,256,1024]{1,2,0:T(8,128)(2,1)S(1)}, bf16[1,256,1024]{1,2,0:T(8,128)(2,1)}, u32[]{:S(2)}) copy-start(bf16[1,256,1024]{1,2,0:T(8,128)(2,1)} %copy-done.15) | copy-start | bytes 1572868
  97.3 8.5 %collective-permute-start.4 = (bf16[128,1024]{0,1:T(8,128)(2,1)S(1)}, bf16[128,1024]{0,1:T(8,128)(2,1)S(1)}, u32[]{:S(2)}, u32[]{:S(2)}) collective-permute-start(bf16[128,1024]{0,1:T(8,128)(2,1)S(1)} %get-tuple-element.188), channel_id=1, source_target_pairs={{0,16},{8,24},{16,0},{24,8},{1,17},{9,25},{17,1},{25,9},{2,18},{10... | collective-permute-start | bytes 786440 | tf_op jit(solution)/shard_map/ppermute | solution.py:108
  98.8 8.2 %collective-permute-start.6 = (bf16[128,1024]{0,1:T(8,128)(2,1)S(1)}, bf16[128,1024]{0,1:T(8,128)(2,1)S(1)}, u32[]{:S(2)}, u32[]{:S(2)}) collective-permute-start(bf16[128,1024]{0,1:T(8,128)(2,1)S(1)} %get-tuple-element.189), channel_id=1, source_target_pairs={{0,8},{8,0},{16,24},{24,16},{1,9},{9,1},{17,25},{25,17},{2,10},{10... | collective-permute-start | bytes 786440 | tf_op jit(solution)/shard_map/ppermute | solution.py:108
  107.2 13.1 %collective-permute-start.7 = (bf16[256,1024]{0,1:T(8,128)(2,1)S(1)}, bf16[256,1024]{0,1:T(8,128)(2,1)S(1)}, u32[]{:S(2)}, u32[]{:S(2)}) collective-permute-start(bf16[256,1024]{0,1:T(8,128)(2,1)S(1)} %pad_maximum_fusion.3), channel_id=1, source_target_pairs={{0,16},{8,24},{16,0},{24,8},{1,17},{9,25},{17,1},{25,9},{2,18},{10... | collective-permute-start | bytes 1572872 | tf_op jit(solution)/shard_map/ppermute | solution.py:108
  107.9 12.9 %collective-permute-start.5 = (bf16[256,1024]{0,1:T(8,128)(2,1)S(1)}, bf16[256,1024]{0,1:T(8,128)(2,1)S(1)}, u32[]{:S(2)}, u32[]{:S(2)}) collective-permute-start(bf16[256,1024]{0,1:T(8,128)(2,1)S(1)} %pad_maximum_fusion.2), channel_id=1, source_target_pairs={{0,8},{8,0},{16,24},{24,16},{1,9},{9,1},{17,25},{25,17},{2,10},{10... | collective-permute-start | bytes 1572872 | tf_op jit(solution)/shard_map/ppermute | solution.py:108
  121.9 199.2 %reduce-scatter.7.cloned.1.call-start = ((), (), s32[]{:S(2)}) async-start(), calls=%async_computation.10 | async-start | bytes 4718592 | tf_op jit(solution)/shard_map/reduce_scatter | solution.py:324
  270.5 100.9 %reduce-scatter.9.cloned.1.call-start = ((), (), s32[]{:S(2)}) async-start(), calls=%async_computation.12 | async-start | bytes 4718592 | tf_op jit(solution)/shard_map/reduce_scatter | solution.py:332
  291.0 12.5 %all-to-all-start.2 = ((f32[8,12,256]{2,1,0:T(8,128)}), f32[8,12,256]{2,1,0:T(8,128)S(1)}, u32[]{:S(2)}, u32[]{:S(2)}) async-start(f32[8,12,256]{2,1,0:T(8,128)} %copy.271), calls=%async_computation.4 | async-start | bytes 262144 | tf_op jit(solution)/shard_map/all_to_all | solution.py:335
  294.3 224.1 %all-reduce.4.cloned.1.call-start = ((), (), s32[]{:S(2)}) async-start(), calls=%async_computation.14 | async-start | bytes 6815744
  305.1 66.3 %copy-start.58 = (pred[256]{0:T(512)(128)(4,1)S(1)}, pred[256]{0:T(512)(128)(4,1)}, u32[]{:S(2)}) copy-start(pred[256]{0:T(512)(128)(4,1)} %copy-done.57) | copy-start | bytes 772
  374.8 13.1 %collective-permute-start.8 = (bf16[256,1024]{0,1:T(8,128)(2,1)}, bf16[256,1024]{0,1:T(8,128)(2,1)S(1)}, u32[]{:S(2)}, u32[]{:S(2)}) collective-permute-start(bf16[256,1024]{0,1:T(8,128)(2,1)} %get-tuple-element.171), channel_id=1, source_target_pairs={{0,8},{8,0},{16,24},{24,16},{1,9},{9,1},{17,25},{25,17},{2,10},{10... | collective-permute-start | bytes 1572872 | tf_op jit(solution)/shard_map/ppermute | solution.py:108
  376.3 15.8 %collective-permute-start.9 = (bf16[256,1024]{0,1:T(8,128)(2,1)}, bf16[256,1024]{0,1:T(8,128)(2,1)}, u32[]{:S(2)}, u32[]{:S(2)}) collective-permute-start(bf16[256,1024]{0,1:T(8,128)(2,1)} %get-tuple-element.171), channel_id=1, source_target_pairs={{0,16},{8,24},{16,0},{24,8},{1,17},{9,25},{17,1},{25,9},{2,18},{10... | collective-permute-start | bytes 1572872 | tf_op jit(solution)/shard_map/ppermute | solution.py:108
  389.4 8.7 %collective-permute-start.10 = (bf16[128,1024]{0,1:T(8,128)(2,1)}, bf16[128,1024]{0,1:T(8,128)(2,1)}, u32[]{:S(2)}, u32[]{:S(2)}) collective-permute-start(bf16[128,1024]{0,1:T(8,128)(2,1)} %slice.261), channel_id=1, source_target_pairs={{0,16},{8,24},{16,0},{24,8},{1,17},{9,25},{17,1},{25,9},{2,18},{10... | collective-permute-start | bytes 786440 | tf_op jit(solution)/shard_map/ppermute | solution.py:108
  393.1 6.7 %collective-permute-start.11 = (bf16[128,1024]{0,1:T(8,128)(2,1)S(1)}, bf16[128,1024]{0,1:T(8,128)(2,1)S(1)}, u32[]{:S(2)}, u32[]{:S(2)}) collective-permute-start(bf16[128,1024]{0,1:T(8,128)(2,1)S(1)} %slice.262), channel_id=1, source_target_pairs={{0,8},{8,0},{16,24},{24,16},{1,9},{9,1},{17,25},{25,17},{2,10},{10... | collective-permute-start | bytes 786440 | tf_op jit(solution)/shard_map/ppermute | solution.py:108
  436.2 156.4 %reduce-scatter.11.cloned.1.call-start = ((), (), s32[]{:S(2)}) async-start(), calls=%async_computation.13 | async-start | bytes 7864320 | tf_op jit(solution)/shard_map/reduce_scatter | solution.py:346
  455.9 6.4 %collective-permute-start.12 = (bf16[128,1024]{0,1:T(8,128)(2,1)S(1)}, bf16[128,1024]{0,1:T(8,128)(2,1)S(1)}, u32[]{:S(2)}, u32[]{:S(2)}) collective-permute-start(bf16[128,1024]{0,1:T(8,128)(2,1)S(1)} %get-tuple-element.184), channel_id=1, source_target_pairs={{0,16},{8,24},{16,0},{24,8},{1,17},{9,25},{17,1},{25,9},{2,18},{10... | collective-permute-start | bytes 786440 | tf_op jit(solution)/shard_map/ppermute | solution.py:108
  457.2 6.4 %collective-permute-start.14 = (bf16[128,1024]{0,1:T(8,128)(2,1)S(1)}, bf16[128,1024]{0,1:T(8,128)(2,1)S(1)}, u32[]{:S(2)}, u32[]{:S(2)}) collective-permute-start(bf16[128,1024]{0,1:T(8,128)(2,1)S(1)} %get-tuple-element.185), channel_id=1, source_target_pairs={{0,8},{8,0},{16,24},{24,16},{1,9},{9,1},{17,25},{25,17},{2,10},{10... | collective-permute-start | bytes 786440 | tf_op jit(solution)/shard_map/ppermute | solution.py:108
  464.5 60.2 %collective-permute-start.15 = (bf16[256,1024]{0,1:T(8,128)(2,1)}, bf16[256,1024]{0,1:T(8,128)(2,1)}, u32[]{:S(2)}, u32[]{:S(2)}) collective-permute-start(bf16[256,1024]{0,1:T(8,128)(2,1)} %pad_maximum_fusion.6), channel_id=1, source_target_pairs={{0,16},{8,24},{16,0},{24,8},{1,17},{9,25},{17,1},{25,9},{2,18},{10... | collective-permute-start | bytes 1572872 | tf_op jit(solution)/shard_map/ppermute | solution.py:108
  466.2 58.6 %collective-permute-start.13 = (bf16[256,1024]{0,1:T(8,128)(2,1)}, bf16[256,1024]{0,1:T(8,128)(2,1)}, u32[]{:S(2)}, u32[]{:S(2)}) collective-permute-start(bf16[256,1024]{0,1:T(8,128)(2,1)} %pad_maximum_fusion.5), channel_id=1, source_target_pairs={{0,8},{8,0},{16,24},{24,16},{1,9},{9,1},{17,25},{25,17},{2,10},{10... | collective-permute-start | bytes 1572872 | tf_op jit(solution)/shard_map/ppermute | solution.py:108
  474.0 50.8 %copy-start.17 = (f32[256,1024]{0,1:T(8,128)S(1)}, f32[256,1024]{0,1:T(8,128)}, u32[]{:S(2)}) copy-start(f32[256,1024]{0,1:T(8,128)} %get-tuple-element.172) | copy-start | bytes 3145732
  520.9 13.5 %all-to-all-start.3 = ((bf16[4,32,1664]{2,1,0:T(8,128)(2,1)}), bf16[4,32,1664]{2,1,0:T(8,128)(2,1)S(1)}, u32[]{:S(2)}, u32[]{:S(2)}) async-start(bf16[4,32,1664]{2,1,0:T(8,128)(2,1)} %dynamic-slice_bitcast_fusion), calls=%async_computation.5 | async-start | bytes 851968 | tf_op jit(solution)/shard_map/all_to_all | solution.py:411
  (59 other events, 301.0 us)
Sparse Core Ops, SparseCore 0:
  29.2 39.8 all-gather.4
  70.8 46.6 all-gather.10
  119.8 68.2 all-gather.8
  190.1 47.8 all-gather.6
  270.6 50.3 reduce-scatter.6
  323.2 48.1 reduce-scatter.8
  436.3 82.0 all-reduce.3
  521.4 71.1 reduce-scatter.10
